TPU v7x, 128 devices: a whole 4x4x4 slice. The times are simulated.
128 devices in a mesh: row: 8 (over z, core), col: 16 (over y, x).
Axes of the slice: x: 4, y: 4, z: 4, core: 2. Of those that a mesh axis runs over, the one named last changes fastest.
Arguments:
- base: bfloat16 [256, 512, 256], P('row', 'col'), may hold values from -6 to 6
- observations: bfloat16 [65536, 128], P(('row', 'col')), may hold values from -6 to 6
- destination: int32 [65536, 1], P(('row', 'col')), may hold values from 0 to 127; in each aligned block of 512 rows (0 to 511, 512 to 1023, ...) at most 8 rows name the same one
- cell_index: int32 [65536], P(('row', 'col')), may hold values from 0 to 1023
- shard_counts: int32 [128], P(('row', 'col')), may hold values from 1 to 512, 49152 in all
- embed_weight: bfloat16 [128, 256], replicated, may hold values from -0.5 to 0.5
- conv_weights: bfloat16 [3, 9, 256, 256], replicated, may hold values from -0.125 to 0.125
- cotangent: bfloat16 [256, 512, 256], P('row', 'col'), may hold values from -6 to 6
Outputs:
- block_out: bfloat16 [256, 512, 256], P('row', 'col')
- base_grad: float32 [256, 512, 256], P('row', 'col')
- conv_grads: float32 [3, 9, 256, 256], replicated
- embed_grad: float32 [128, 256], replicated
Inputs may be any that keep to these rules, and one draw needn't show every extreme that they name: `destination`: among the 512 rows of one ingestion shard, live or not, at most 8 name the same tile. `shard_counts`: rows of a shard at positions from its count on are ignored.
All inputs are finite; a program needn't handle non-finite values.
Results may differ from a plain program's by a relative error of at most 0.017.
Values may be sent and summed in bfloat16 or wider, within the bound.
A program may use at most 128 MiB of HBM per device.

v0:
```python
import math

import jax
import jax.numpy as jnp
from jax import lax
from jax.experimental import pallas as pl
from jax.experimental.pallas import tpu as pltpu
from jax.sharding import PartitionSpec as P

MESH = pl.DeviceIdType.MESH
BF = jnp.bfloat16
F32 = jnp.float32
ORDERS = (("x", "y", "z"), ("y", "z", "x"), ("z", "x", "y"))
EXT = 48
DEVICES = 128


def f32(value):
    return value.astype(F32)


def low(value):
    return value.astype(BF)


class Place:
    def __init__(self):
        self.row, self.col = lax.axis_index("row"), lax.axis_index("col")
        self.index = self.row * 16 + self.col
        self.core = lax.rem(self.row, 2)
        self.at = {"z": lax.div(self.row, 2), "y": lax.div(self.col, 4), "x": lax.rem(self.col, 4)}

    def device(self, **changed):
        at = {**self.at, "core": self.core, **changed}
        return (at["z"] * 2 + at["core"], at["y"] * 4 + at["x"])

    def other(self, axis, step):
        return lax.rem(self.at[axis] + step, 4)

    def sibling(self):
        return self.device(core=1 - self.core)

    def grid_neighbour(self, down, right):
        return (lax.rem(self.row + 8 + down, 8), lax.rem(self.col + 16 + right, 16))

    def by_step(self, step):
        number = lax.rem(self.index + step, DEVICES)
        return number, (lax.div(number, 16), lax.rem(number, 16))


def remote(src, dst, sems, device):
    return pltpu.make_async_remote_copy(
        src_ref=src, dst_ref=dst, send_sem=sems[0], recv_sem=sems[1], device_id=device, device_id_type=MESH
    )


def part_of(index, size):
    return pl.ds(pl.multiple_of(index * size, size), size)


class KernelSum:
    def __init__(self, place, layer, refs):
        self.place, self.layer, self.refs = place, layer, refs
        self.lanes = part_of(place.core, 128)
        self.steps = [
            self.swap, self.scatter_a, self.scatter_b, self.share_c, self.gather_b, self.gather_a,
            self.swap_back, self.end,
        ]

    def swap_copy(self, back):
        r, l, core = self.refs, self.layer, self.place.core
        sems = r.swap_send.at[l, back], r.swap_recv.at[l, back]
        if back:
            mine = r.out.at[l, :, :, :, :, self.lanes]
            return remote(mine, mine, sems, self.place.sibling())
        return remote(r.part.at[l, 1 - core], r.sib.at[l], sems, self.place.sibling())

    def copies(self, phase):
        r, l = self.refs, self.layer
        result = []
        for group, (a, b, c) in enumerate(ORDERS):
            axis = (a, b, c, b, a)[phase]
            mine = self.place.at[axis]
            for step in (1, 2, 3):
                to = self.place.other(axis, step)
                src, dst = [
                    lambda: (r.a_own.at[l, group, part_of(to, 192)], r.a_in.at[l, group, step - 1]),
                    lambda: (r.b_own.at[l, group, to], r.b_in.at[l, group, step - 1]),
                    lambda: (r.c_all.at[l, group, mine], r.c_all.at[l, group, mine]),
                    lambda: (r.b_res.at[l, group, mine], r.b_res.at[l, group, mine]),
                    lambda: (r.b_res.at[l, group], r.out.at[l, group, mine, :, :, self.lanes]),
                ][phase]()
                sems = r.send.at[l, group, phase, step - 1], r.recv.at[l, group, phase, step - 1]
                result.append(remote(src, dst, sems, self.place.device(**{axis: to})))
        return result

    def start(self, phase):
        for copy in self.copies(phase):
            copy.start()

    def wait(self, phase):
        for copy in self.copies(phase):
            copy.wait()

    def swap(self):
        self.swap_copy(0).start()

    def scatter_a(self):
        r, l, core = self.refs, self.layer, self.place.core
        self.swap_copy(0).wait()
        for group in range(3):
            r.a_own[l, group] = low(f32(r.part[l, core, group]) + f32(r.sib[l, group]))
        self.start(0)

    def scatter_b(self):
        r, l = self.refs, self.layer
        self.wait(0)
        for group, (a, b, c) in enumerate(ORDERS):
            total = f32(r.a_own[l, group, part_of(self.place.at[a], 192)])
            for step in range(3):
                total += f32(r.a_in[l, group, step])
            r.b_own[l, group] = low(total).reshape(4, 48, 128)
        self.start(1)

    def share_c(self):
        r, l = self.refs, self.layer
        self.wait(1)
        for group, (a, b, c) in enumerate(ORDERS):
            total = f32(r.b_own[l, group, self.place.at[b]])
            for step in range(3):
                total += f32(r.b_in[l, group, step])
            r.c_all[l, group, self.place.at[c]] = low(total)
        self.start(2)

    def gather_b(self):
        r, l = self.refs, self.layer
        self.wait(2)
        for group, (a, b, c) in enumerate(ORDERS):
            total = f32(r.c_all[l, group, 0])
            for index in (1, 2, 3):
                total += f32(r.c_all[l, group, index])
            r.b_res[l, group, self.place.at[b]] = low(total)
        self.start(3)

    def gather_a(self):
        r, l = self.refs, self.layer
        self.wait(3)
        self.start(4)
        for group, (a, b, c) in enumerate(ORDERS):
            r.out[l, group, self.place.at[a], :, :, self.lanes] = r.b_res[l, group]

    def swap_back(self):
        self.wait(4)
        self.swap_copy(1).start()

    def end(self):
        self.swap_copy(1).wait()


class EmbedSum(KernelSum):
    def __init__(self, place, refs):
        self.place, self.refs = place, refs
        self.lanes = part_of(place.core, 128)
        self.steps = [self.swap, self.scatter, self.share_y, self.share_x, self.gather, self.swap_back, self.end]

    def swap_copy(self, back):
        r, core = self.refs, self.place.core
        sems = r.e_swap_send.at[back], r.e_swap_recv.at[back]
        if back:
            mine = r.e_out.at[:, :, self.lanes]
            return remote(mine, mine, sems, self.place.sibling())
        return remote(r.e_part.at[1 - core], r.e_sib, sems, self.place.sibling())

    def copies(self, phase):
        r = self.refs
        axis = ("z", "y", "x", "z")[phase]
        mine, result = self.place.at[axis], []
        for step in (1, 2, 3):
            to = self.place.other(axis, step)
            src, dst = [
                lambda: (r.e_own.at[to], r.e_in.at[step - 1]),
                lambda: (r.e_y.at[mine], r.e_y.at[mine]),
                lambda: (r.e_x.at[mine], r.e_x.at[mine]),
                lambda: (r.e_res, r.e_out.at[mine, :, self.lanes]),
            ][phase]()
            sems = r.e_send.at[phase, step - 1], r.e_recv.at[phase, step - 1]
            result.append(remote(src, dst, sems, self.place.device(**{axis: to})))
        return result

    def scatter(self):
        r = self.refs
        self.swap_copy(0).wait()
        r.e_own[...] = low(f32(r.e_part[self.place.core]) + f32(r.e_sib[...]))
        self.start(0)

    def share_y(self):
        r = self.refs
        self.wait(0)
        total = f32(r.e_own[self.place.at["z"]])
        for step in range(3):
            total += f32(r.e_in[step])
        r.e_y[self.place.at["y"]] = low(total)
        self.start(1)

    def share_x(self):
        r = self.refs
        self.wait(1)
        total = f32(r.e_y[0])
        for index in (1, 2, 3):
            total += f32(r.e_y[index])
        r.e_x[self.place.at["x"]] = low(total)
        self.start(2)

    def gather(self):
        r = self.refs
        self.wait(2)
        total = f32(r.e_x[0])
        for index in (1, 2, 3):
            total += f32(r.e_x[index])
        r.e_res[...] = low(total)
        self.start(3)
        r.e_out[self.place.at["z"], :, self.lanes] = low(total)

    def swap_back(self):
        self.wait(3)
        self.swap_copy(1).start()


def sigmoid(x):
    return 0.5 * jnp.tanh(0.5 * x) + 0.5


def silu_slope(hidden):
    sig = sigmoid(hidden)
    return sig * (1.0 + hidden * (1.0 - sig))


SIDES = ((0, -1), (0, 1), (-1, -1), (-1, 1), (1, -1), (1, 1))


class Halo:
    def __init__(self, place, refs, which, ext):
        self.place, self.refs, self.which, self.ext = place, refs, which, ext

    def copies(self):
        r, ext, result = self.refs, self.ext, []
        up, down = ext.at[8:16, 0:32], ext.at[32:40, 0:32]
        pairs = [((-1, 0), up, ext.at[40:48, 0:32]), ((1, 0), down, ext.at[0:8, 0:32])]
        for number, side in enumerate(SIDES):
            rows = part_of(number * 1, 256) if number < 2 else pl.ds(512 + (number - 2) * 64, 64)
            pairs.append((side, r.strip_out.at[self.which, rows], r.strip_in.at[self.which, rows]))
        for number, (side, src, dst) in enumerate(pairs):
            sems = r.halo_send.at[self.which, number], r.halo_recv.at[self.which, number]
            result.append(remote(src, dst, sems, self.place.grid_neighbour(*side)))
        return result

    def rows_of(self, number):
        return slice(number * 256, number * 256 + 256) if number < 2 else slice(512 + (number - 2) * 64, 576 + (number - 2) * 64)

    def start(self):
        r, ext = self.refs, self.ext
        for number, (down, right) in enumerate(SIDES):
            rows = {0: slice(8, 40), -1: slice(8, 16), 1: slice(32, 40)}[down]
            half = f32(ext[rows, 0:16] if right < 0 else ext[rows, 16:32])
            strip = half[:, 0:8] if right < 0 else half[:, 8:16]
            r.strip_out[self.which, self.rows_of(number)] = low(strip.reshape(-1, 256))
        for copy in self.copies():
            copy.start()

    def end(self):
        r, ext = self.refs, self.ext
        for copy in self.copies():
            copy.wait()
        for down, rows in ((0, slice(8, 40)), (1, slice(0, 8)), (-1, slice(40, 48))):
            strips = []
            for right in (-1, 1):
                strip = f32(r.strip_in[self.which, self.rows_of(SIDES.index((down, right)))])
                strips.append(strip.reshape(-1, 8, 256))
            ext[rows, 32:48] = low(jnp.concatenate(strips, axis=1))


class Stations:
    def __init__(self, place, refs):
        self.place, self.refs = place, refs

    def route(self):
        r = self.refs
        target = r.meta[:, 0:1]
        cell = r.meta[:, 1:2]
        lane = lax.broadcasted_iota(jnp.int32, (512, DEVICES), 1)
        marks = jnp.where(target == lane, 1.0, 0.0)
        earlier = lax.broadcasted_iota(jnp.int32, (512, 512), 0) > lax.broadcasted_iota(jnp.int32, (512, 512), 1)
        before = jnp.dot(low(jnp.where(earlier, 1.0, 0.0)), low(marks), preferred_element_type=F32)
        rank = jnp.sum(before * marks, axis=1, keepdims=True)
        slot = f32(target) * 8.0 + rank
        picks = low(jnp.where(slot == f32(lax.broadcasted_iota(jnp.int32, (512, 1024), 1)), 1.0, 0.0))
        where = jnp.where(lane < 64, cell >> 5, cell & 31)
        info = low(f32(jnp.where(cell >= 0, where + 1, 0)))
        across = (((0,), (0,)), ((), ()))
        rows = lax.dot_general(picks, r.obs[...], across, preferred_element_type=F32).reshape(DEVICES, 8, 128)
        cells = lax.dot_general(picks, info, across, preferred_element_type=F32).reshape(DEVICES, 8, 128)
        r.st_out[...] = low(jnp.concatenate([rows, cells], axis=1))

    def send(self):
        r, place = self.refs, self.place

        def one(step, carry):
            number, device = place.by_step(step)
            remote(r.st_out.at[number], r.st_in.at[place.index], (r.st_send, r.st_recv), device).start()
            return carry

        lax.fori_loop(1, DEVICES, one, 0)
        r.st_in[place.index] = r.st_out[place.index]

    def receive(self):
        r = self.refs
        all_in = r.st_in.at[pl.ds(0, DEVICES - 1)]
        remote(all_in, all_in, (r.st_send, r.st_recv), self.place.by_step(1)[1]).wait()
        blocks = f32(r.st_in[...])
        r.rows[...] = low(blocks[:, 0:8].reshape(1024, 128))
        info = blocks[:, 8:16].reshape(1024, 128)
        r.cell_col[...] = info[:, 0:1] * 32.0 + info[:, 64:65] - 33.0
        turned = info.T
        cell_row = turned[0:1, :] * 32.0 + turned[64:65, :] - 33.0
        embedded = low(jnp.dot(r.rows[...], r.embed[...], preferred_element_type=F32))
        for part in range(4):
            cells = f32(lax.broadcasted_iota(jnp.int32, (256, 1024), 0) + part * 256)
            picks = low(jnp.where(cells == cell_row, 1.0, 0.0))
            placed = jnp.dot(picks, embedded, preferred_element_type=F32).reshape(8, 32, 256)
            own = slice(part * 8, part * 8 + 8)
            r.hid[0, part * 8 + 8 : part * 8 + 16, 0:32] = low(f32(r.base[own]) + placed)

    def gradient(self, grad_low):
        r = self.refs
        for part in range(2):
            rows = slice(part * 512, part * 512 + 512)
            cells = f32(lax.broadcasted_iota(jnp.int32, (512, 1024), 1))
            picks = low(jnp.where(cells == r.cell_col[rows], 1.0, 0.0))
            picked = low(jnp.dot(picks, grad_low, preferred_element_type=F32))
            total = lax.dot_general(r.rows[rows], picked, (((0,), (0,)), ((), ())), preferred_element_type=F32)
            yield total


def greet():
    place, barrier = Place(), pltpu.get_barrier_semaphore()

    def one(step, carry):
        pl.semaphore_signal(barrier, inc=1, device_id=place.by_step(step)[1], device_id_type=MESH)
        return carry

    lax.fori_loop(1, DEVICES, one, 0)
    return lambda: pl.semaphore_wait(barrier, DEVICES - 1)


class Convs:
    def __init__(self, place, refs):
        self.place, self.refs = place, refs

    def inside(self, first, rows):
        row = lax.broadcasted_iota(jnp.int32, (rows, EXT, 256), 0) + (first - 8 + self.place.row * 32)
        col = lax.broadcasted_iota(jnp.int32, (rows, EXT, 256), 1)
        col = jnp.where(col < 40, col, col - EXT) + self.place.col * 32
        return (row >= 0) & (row < 256) & (col >= 0) & (col < 512)

    def spread(self, value_of, out, spacing, sign, rows):
        first, last, size = rows

        def one(step, carry):
            row = first + step * size
            value = jnp.where(self.inside(row, size), value_of(row, size), 0.0)
            out[1, pl.ds(row, size)] = low(value)
            out[1 - sign, pl.ds(row, size)] = low(jnp.roll(value, spacing, axis=1))
            out[1 + sign, pl.ds(row, size)] = low(jnp.roll(value, -spacing, axis=1))
            return carry

        lax.fori_loop(0, (last - first) // size, one, 0)

    def activate(self, layer, rows):
        hid = self.refs.hid.at[layer]

        def value(row, size):
            x = f32(hid[pl.ds(row, size)])
            return x * sigmoid(x)

        self.spread(value, self.refs.act.at[layer], 2**layer, 1, rows)

    def taps(self, source, weights, row, size, width, spacing, sign, turned):
        total = None
        for i in range(3):
            for j in range(3):
                cells = source[j, pl.ds(row + sign * (i - 1) * spacing, size), 0:width].reshape(size * width, 256)
                contract = (((1,), (1 if turned else 0,)), ((), ()))
                term = lax.dot_general(cells, weights[3 * i + j], contract, preferred_element_type=F32)
                total = term if total is None else total + term
        return total.reshape(size, width, 256)

    def forward(self, layer, rows, width=EXT):
        r, (first, last, size) = self.refs, rows

        def one(step, carry):
            row = first + step * size
            update = self.taps(r.act.at[layer], r.weights.at[layer], row, size, width, 2**layer, 1, False)
            result = low(f32(r.hid[layer, pl.ds(row, size), 0:width]) + update)
            if layer == 2:
                r.block_out[pl.ds(row - 8, size)] = result
            else:
                r.hid[layer + 1, pl.ds(row, size)] = result
            return carry

        lax.fori_loop(0, (last - first) // size, one, 0)

    def kernel(self, layer):
        r, spacing = self.refs, 2**layer
        grad = r.grad_low[1, 8:40, 0:32].reshape(1024, 256)

        def one(j, carry):
            for i in range(3):
                row = 8 + (i - 1) * spacing
                cells = r.act[layer, j, row : row + 32, 0:32].reshape(1024, 256)
                total = lax.dot_general(cells, grad, (((0,), (0,)), ((), ())), preferred_element_type=F32)
                for half in range(2):
                    r.part[layer, half, i, part_of(j, 256)] = low(total[:, half * 128 : half * 128 + 128])
            return carry

        lax.fori_loop(0, 3, one, 0)

    def back(self, layer, rows, width=EXT):
        r, (first, last, size) = self.refs, rows

        def one(step, carry):
            row = first + step * size
            update = self.taps(r.grad_low, r.weights.at[layer], row, size, width, 2**layer, -1, True)
            before = f32(r.cot[pl.ds(row, size)]) if layer == 2 else r.grad[pl.ds(row, size), 0:width]
            result = before + update * silu_slope(f32(r.hid[layer, pl.ds(row, size), 0:width]))
            if layer == 0:
                r.base_grad[pl.ds(row - 8, size)] = result
            else:
                r.grad[pl.ds(row, size)] = result
            return carry

        lax.fori_loop(0, (last - first) // size, one, 0)

    def spread_grad(self, layer, rows):
        r = self.refs

        def value(row, size):
            return f32(r.cot[pl.ds(row, size)]) if layer == 2 else r.grad[pl.ds(row, size)]

        self.spread(value, r.grad_low, 2**layer, -1, rows)


class Refs:
    def __init__(self, names, refs):
        self.__dict__.update(zip(names, refs))


def whole_kernel(names, *refs):
    r = Refs(names, refs)
    place = Place()
    finish_greeting = greet()
    fetch = pltpu.make_async_copy(r.weights_hbm, r.weights, r.fetch)
    fetch.start()
    stations, convs = Stations(place, r), Convs(place, r)
    stations.route()
    r.cot[8:40, 0:32] = r.cotangent[...]
    halo_cot, halo_hid = Halo(place, r, 0, r.cot), Halo(place, r, 1, r.hid.at[0])
    finish_greeting()
    stations.send()
    halo_cot.start()
    stations.receive()
    halo_hid.start()
    halo_cot.end()
    convs.spread_grad(2, (0, 48, 4))
    fetch.wait()
    halo_hid.end()
    convs.activate(0, (0, 48, 4))
    convs.forward(0, (2, 46, 11))
    convs.activate(1, (2, 46, 4))
    convs.forward(1, (4, 44, 10))
    convs.activate(2, (4, 44, 4))
    convs.forward(2, (8, 40, 16), 32)

    sums = {layer: KernelSum(place, layer, r).steps for layer in range(3)}
    sums["e"] = EmbedSum(place, r).steps

    def step(*which):
        for name in which:
            sums[name].pop(0)()

    convs.kernel(2)
    step(2)
    convs.back(2, (4, 24, 10))
    step(2)
    convs.back(2, (24, 44, 10))
    step(2)
    convs.spread_grad(1, (4, 44, 4))
    convs.kernel(1)
    step(2, 1)
    convs.back(1, (6, 24, 9))
    step(2, 1)
    convs.back(1, (24, 42, 9))
    step(2, 1)
    convs.spread_grad(0, (6, 42, 4))
    convs.kernel(0)
    step(2, 1, 0)
    convs.back(0, (8, 40, 16), 32)
    step(2, 1, 0)
    grad_low = low(r.base_grad[...].reshape(1024, 256))
    first, second = stations.gradient(grad_low)
    total = first + second
    for half in range(2):
        r.e_part[half] = low(total[:, half * 128 : half * 128 + 128]).reshape(4, 32, 128)
    step("e")
    while any(sums.values()):
        step(*[name for name in (1, 0, "e") if sums[name]])


SUM_SCRATCH = dict(
    part=pltpu.VMEM((3, 2, 3, 768, 128), BF),
    sib=pltpu.VMEM((3, 3, 768, 128), BF),
    a_own=pltpu.VMEM((3, 3, 768, 128), BF),
    a_in=pltpu.VMEM((3, 3, 3, 192, 128), BF),
    b_own=pltpu.VMEM((3, 3, 4, 48, 128), BF),
    b_in=pltpu.VMEM((3, 3, 3, 48, 128), BF),
    c_all=pltpu.VMEM((3, 3, 4, 48, 128), BF),
    b_res=pltpu.VMEM((3, 3, 4, 48, 128), BF),
    e_part=pltpu.VMEM((2, 4, 32, 128), BF),
    e_sib=pltpu.VMEM((4, 32, 128), BF),
    e_own=pltpu.VMEM((4, 32, 128), BF),
    e_in=pltpu.VMEM((3, 32, 128), BF),
    e_y=pltpu.VMEM((4, 32, 128), BF),
    e_x=pltpu.VMEM((4, 32, 128), BF),
    e_res=pltpu.VMEM((32, 128), BF),
    send=pltpu.SemaphoreType.DMA((3, 3, 5, 3)),
    recv=pltpu.SemaphoreType.DMA((3, 3, 5, 3)),
    swap_send=pltpu.SemaphoreType.DMA((3, 2)),
    swap_recv=pltpu.SemaphoreType.DMA((3, 2)),
    e_send=pltpu.SemaphoreType.DMA((4, 3)),
    e_recv=pltpu.SemaphoreType.DMA((4, 3)),
    e_swap_send=pltpu.SemaphoreType.DMA((2,)),
    e_swap_recv=pltpu.SemaphoreType.DMA((2,)),
)
SCRATCH = dict(
    SUM_SCRATCH,
    weights=pltpu.VMEM((3, 9, 256, 256), BF),
    fetch=pltpu.SemaphoreType.DMA,
    st_out=pltpu.VMEM((DEVICES, 16, 128), BF),
    st_in=pltpu.VMEM((DEVICES, 16, 128), BF),
    st_send=pltpu.SemaphoreType.DMA,
    st_recv=pltpu.SemaphoreType.DMA,
    rows=pltpu.VMEM((1024, 128), BF),
    cell_col=pltpu.VMEM((1024, 1), F32),
    cot=pltpu.VMEM((EXT, EXT, 256), BF),
    hid=pltpu.VMEM((3, EXT, EXT, 256), BF),
    act=pltpu.VMEM((3, 3, EXT, EXT, 256), BF),
    grad_low=pltpu.VMEM((3, EXT, EXT, 256), BF),
    grad=pltpu.VMEM((EXT, EXT, 256), F32),
    strip_out=pltpu.VMEM((2, 768, 256), BF),
    strip_in=pltpu.VMEM((2, 768, 256), BF),
    halo_send=pltpu.SemaphoreType.DMA((2, 8)),
    halo_recv=pltpu.SemaphoreType.DMA((2, 8)),
)
INPUTS = ("base", "obs", "meta", "embed", "weights_hbm", "cotangent")
OUTPUTS = ("block_out", "base_grad", "out", "e_out")


def local(
    base, observations, destination, cell_index, shard_counts, embed_weight, conv_weights, cotangent
):
    live = jnp.arange(512, dtype=jnp.int32) < shard_counts[0]
    meta = jnp.concatenate([destination, jnp.where(live, cell_index, -1)[:, None]], axis=1)
    vmem, anywhere = pl.BlockSpec(memory_space=pltpu.VMEM), pl.BlockSpec(memory_space=pl.ANY)
    names = INPUTS + OUTPUTS + tuple(SCRATCH)
    block_out, base_grad, total, e_total = pl.pallas_call(
        lambda *refs: whole_kernel(names, *refs),
        out_shape=[
            jax.ShapeDtypeStruct((32, 32, 256), BF),
            jax.ShapeDtypeStruct((32, 32, 256), F32),
            jax.ShapeDtypeStruct((3, 3, 4, 4, 48, 256), BF),
            jax.ShapeDtypeStruct((4, 32, 256), BF),
        ],
        in_specs=[vmem, vmem, vmem, vmem, anywhere, vmem],
        out_specs=[vmem, vmem, vmem, vmem],
        scratch_shapes=list(SCRATCH.values()),
        compiler_params=pltpu.CompilerParams(
            collective_id=0, has_side_effects=True, vmem_limit_bytes=60 * 2**20
        ),
        name="station_block",
    )(base, observations, meta, embed_weight, conv_weights, cotangent)
    scale = 1.0 / math.sqrt(131072)
    conv_grads = total.reshape(3, 9, 256, 256).astype(F32) * scale
    embed_grad = e_total.reshape(128, 256).astype(F32) * scale
    return (block_out, base_grad, conv_grads, embed_grad)


def solution(mesh):
    return jax.shard_map(
        local,
        mesh=mesh,
        in_specs=(
            P("row", "col", None),
            P(("row", "col"), None),
            P(("row", "col"), None),
            P(("row", "col")),
            P(("row", "col")),
            P(),
            P(),
            P("row", "col", None),
        ),
        out_specs=(P("row", "col", None), P("row", "col", None), P(), P()),
        check_vma=False,
    )
```

profile of v0, /device:TPU:1, one launch (start us, length us, event | category | flops | bytes accessed | tf_op | source)
XLA Modules:
  0.0 113.0 jit_solution(9674368762439586368)
XLA Ops:
  1.3 0.7 fusion
  2.0 0.7 pad_add_fusion
  2.7 0.9 copy.15.refs_2_
  3.5 100.9 %station_block.1 = (bf16[32,32,256]{2,1,0:T(8,128)(2,1)}, f32[32,32,256]{2,1,0:T(8,128)}, bf16[3,3,4,4,48,256]{5,4,3,2,1,0:T(8,128)(2,1)}, bf16[4,32,256]{2,1,0:T(8,128)(2,1)}) custom-call(bf16[32,32,256]{2,1,0:T(8,128)(2,1)} %refs_0_.1, bf16[512,128]{1,0:T(8,128)(2,1)} %refs_1_.1, s32[512,2]{1,0:T(8,128)} %copy.15.refs_2_, bf16[128,256]{1,0:T(8,128)(2,1)} %refs_3_.1, ...), custom_call_target="tpu_custom_call" | custom-call | tf_op jit(solution)/shard_map/station_block/pallas_call | solution.py:574
  104.4 0.0 copy-start.2
  104.4 0.0 copy-start.1
  104.4 0.0 copy-start
  104.4 6.1 %convert_multiply_fusion = f32[3,3,4,4,48,256]{5,4,3,2,1,0:T(8,128)} fusion(bf16[3,3,4,4,48,256]{5,4,3,2,1,0:T(8,128)(2,1)} %get-tuple-element.10), kind=kLoop, calls=%fused_computation | loop fusion | flops 3538944 | bytes 10616832 | tf_op jit(solution)/shard_map/mul | solution.py:591
  110.5 0.0 copy-done.2
  110.5 0.7 convert_multiply_fusion.1
  111.2 0.0 copy-done.1
  111.2 0.8 copy.19
  112.0 0.0 copy-done
  112.0 1.0 copy.20
Async XLA Ops:
  104.4 6.1 %copy-start.2 = (bf16[4,32,256]{2,1,0:T(8,128)(2,1)S(1)}, bf16[4,32,256]{2,1,0:T(8,128)(2,1)}, u32[]{:S(2)}) copy-start(bf16[4,32,256]{2,1,0:T(8,128)(2,1)} %get-tuple-element.11) | copy-start | bytes 196612
  104.4 6.8 %copy-start.1 = (bf16[32,32,256]{2,1,0:T(8,128)(2,1)S(1)}, bf16[32,32,256]{2,1,0:T(8,128)(2,1)}, u32[]{:S(2)}) copy-start(bf16[32,32,256]{2,1,0:T(8,128)(2,1)} %get-tuple-element.16) | copy-start | bytes 1572868
  104.4 7.6 %copy-start = (f32[32,32,256]{2,1,0:T(8,128)S(1)}, f32[32,32,256]{2,1,0:T(8,128)}, u32[]{:S(2)}) copy-start(f32[32,32,256]{2,1,0:T(8,128)} %get-tuple-element.17) | copy-start | bytes 3145732
where the time goes:
time: 113 us
  Pallas kernels  101 us (89%)
  other arithmetic  8.15 us (7%)
  local copies, waits for them, and re-layouts  2.64 us (2%)
  between operations  1.31 us (1%)
    pallas_call x1, Pallas kernels, local(): pl.pallas_call(lambda *refs: whole_kernel(names, *refs), out_shape=[jax.S...  101 us
    mul x1, other arithmetic, local(): conv_grads = total.reshape(3, 9, 256, 256).astype(F32) * scale  6.1 us

commit v1 on v0

--- a/solution.py
+++ b/solution.py
@@ -157,11 +157,68 @@
         self.swap_copy(1).wait()
 
 
+class PlaneSum(KernelSum):
+    def __init__(self, place, layer, refs):
+        super().__init__(place, layer, refs)
+        self.steps = [self.swap, self.scatter, self.share_c, self.gather_b, self.swap_back, self.end]
+
+    def pieces(self, group):
+        a, b, _ = ORDERS[group]
+        for step in range(1, 16):
+            to = {a: self.place.other(a, step // 4), b: self.place.other(b, step % 4)}
+            yield step - 1, to[a], to[b], self.place.device(**to)
+
+    def plane_wait(self, phase):
+        r = self.refs
+        for group in range(3):
+            whole = r.p_in.at[group]
+            remote(whole, whole, (r.p_send.at[phase, group], r.p_recv.at[phase, group]), self.place.sibling()).wait()
+
+    def scatter(self):
+        r, l, core = self.refs, self.layer, self.place.core
+        self.swap_copy(0).wait()
+        for group in range(3):
+            r.a_own[l, group] = low(f32(r.part[l, core, group]) + f32(r.sib[l, group]))
+        for group in range(3):
+            sems = r.p_send.at[0, group], r.p_recv.at[0, group]
+            for slot, to_a, to_b, device in self.pieces(group):
+                piece = r.a_own.at[l, group, part_of(to_a * 4 + to_b, 48)]
+                remote(piece, r.p_in.at[group, slot], sems, device).start()
+
+    def share_c(self):
+        r, l = self.refs, self.layer
+        self.plane_wait(0)
+        for group, (a, b, c) in enumerate(ORDERS):
+            total = f32(r.a_own[l, group, part_of(self.place.at[a] * 4 + self.place.at[b], 48)])
+            for slot in range(15):
+                total += f32(r.p_in[group, slot])
+            r.c_all[l, group, self.place.at[c]] = low(total)
+        self.start(2)
+
+    def gather_b(self):
+        r, l = self.refs, self.layer
+        self.wait(2)
+        for group, (a, b, c) in enumerate(ORDERS):
+            total = f32(r.c_all[l, group, 0])
+            for index in (1, 2, 3):
+                total += f32(r.c_all[l, group, index])
+            mine = r.out.at[l, group, self.place.at[a], self.place.at[b], :, self.lanes]
+            r.b_res[l, group, 0] = low(total)
+            sems = r.p_send.at[1, group], r.p_recv.at[1, group]
+            for _, _, _, device in self.pieces(group):
+                remote(r.b_res.at[l, group, 0], mine, sems, device).start()
+            mine[...] = low(total)
+
+    def swap_back(self):
+        self.plane_wait(1)
+        self.swap_copy(1).start()
+
+
 class EmbedSum(KernelSum):
     def __init__(self, place, refs):
         self.place, self.refs = place, refs
         self.lanes = part_of(place.core, 128)
-        self.steps = [self.swap, self.scatter, self.share_y, self.share_x, self.gather, self.swap_back, self.end]
+        self.steps = [self.swap, self.scatter, self.share, self.gather, self.swap_back, self.end]
 
     def swap_copy(self, back):
         r, core = self.refs, self.place.core
@@ -172,19 +229,12 @@
         return remote(r.e_part.at[1 - core], r.e_sib, sems, self.place.sibling())
 
     def copies(self, phase):
-        r = self.refs
-        axis = ("z", "y", "x", "z")[phase]
-        mine, result = self.place.at[axis], []
+        r, mine, result = self.refs, self.place.at["z"], []
         for step in (1, 2, 3):
-            to = self.place.other(axis, step)
-            src, dst = [
-                lambda: (r.e_own.at[to], r.e_in.at[step - 1]),
-                lambda: (r.e_y.at[mine], r.e_y.at[mine]),
-                lambda: (r.e_x.at[mine], r.e_x.at[mine]),
-                lambda: (r.e_res, r.e_out.at[mine, :, self.lanes]),
-            ][phase]()
+            to = self.place.other("z", step)
+            src, dst = (r.e_own.at[to], r.e_in.at[step - 1]) if phase == 0 else (r.e_res, r.e_out.at[mine, :, self.lanes])
             sems = r.e_send.at[phase, step - 1], r.e_recv.at[phase, step - 1]
-            result.append(remote(src, dst, sems, self.place.device(**{axis: to})))
+            result.append(remote(src, dst, sems, self.place.device(z=to)))
         return result
 
     def scatter(self):
@@ -193,36 +243,31 @@
         r.e_own[...] = low(f32(r.e_part[self.place.core]) + f32(r.e_sib[...]))
         self.start(0)
 
-    def share_y(self):
+    def share(self):
         r = self.refs
         self.wait(0)
         total = f32(r.e_own[self.place.at["z"]])
         for step in range(3):
             total += f32(r.e_in[step])
-        r.e_y[self.place.at["y"]] = low(total)
-        self.start(1)
-
-    def share_x(self):
-        r = self.refs
-        self.wait(1)
-        total = f32(r.e_y[0])
-        for index in (1, 2, 3):
-            total += f32(r.e_y[index])
-        r.e_x[self.place.at["x"]] = low(total)
-        self.start(2)
+        r.e_plane[self.place.col] = low(total)
+        mine = r.e_plane.at[self.place.col]
+        for step in range(1, 16):
+            device = (self.place.row, lax.rem(self.place.col + step, 16))
+            remote(mine, mine, (r.e_plane_send, r.e_plane_recv), device).start()
 
     def gather(self):
         r = self.refs
-        self.wait(2)
-        total = f32(r.e_x[0])
-        for index in (1, 2, 3):
-            total += f32(r.e_x[index])
+        others = r.e_plane.at[0:15]
+        remote(others, others, (r.e_plane_send, r.e_plane_recv), self.place.sibling()).wait()
+        total = f32(r.e_plane[0])
+        for index in range(1, 16):
+            total += f32(r.e_plane[index])
         r.e_res[...] = low(total)
-        self.start(3)
+        self.start(1)
         r.e_out[self.place.at["z"], :, self.lanes] = low(total)
 
     def swap_back(self):
-        self.wait(3)
+        self.wait(1)
         self.swap_copy(1).start()
 
 
@@ -285,17 +330,19 @@
 
     def route(self):
         r = self.refs
-        target = r.meta[:, 0:1]
-        cell = r.meta[:, 1:2]
         lane = lax.broadcasted_iota(jnp.int32, (512, DEVICES), 1)
-        marks = jnp.where(target == lane, 1.0, 0.0)
+        target = jnp.broadcast_to(f32(r.target[...]), (128, 512)).T
+        marks = jnp.where(target == f32(lane), 1.0, 0.0)
+        position = lax.broadcasted_iota(jnp.int32, (1, 512), 1)
+        cell = jnp.where(position < r.count[0], r.cell[...], -1)
+        halves = lax.broadcasted_iota(jnp.int32, (128, 512), 0) < 64
+        where = jnp.where(halves, cell >> 5, cell & 31)
+        info = low(f32(jnp.where(cell >= 0, where + 1, 0)).T)
         earlier = lax.broadcasted_iota(jnp.int32, (512, 512), 0) > lax.broadcasted_iota(jnp.int32, (512, 512), 1)
         before = jnp.dot(low(jnp.where(earlier, 1.0, 0.0)), low(marks), preferred_element_type=F32)
         rank = jnp.sum(before * marks, axis=1, keepdims=True)
-        slot = f32(target) * 8.0 + rank
+        slot = target[:, 0:1] * 8.0 + rank
         picks = low(jnp.where(slot == f32(lax.broadcasted_iota(jnp.int32, (512, 1024), 1)), 1.0, 0.0))
-        where = jnp.where(lane < 64, cell >> 5, cell & 31)
-        info = low(f32(jnp.where(cell >= 0, where + 1, 0)))
         across = (((0,), (0,)), ((), ()))
         rows = lax.dot_general(picks, r.obs[...], across, preferred_element_type=F32).reshape(DEVICES, 8, 128)
         cells = lax.dot_general(picks, info, across, preferred_element_type=F32).reshape(DEVICES, 8, 128)
@@ -458,29 +505,40 @@
     r = Refs(names, refs)
     place = Place()
     finish_greeting = greet()
-    fetch = pltpu.make_async_copy(r.weights_hbm, r.weights, r.fetch)
-    fetch.start()
+    fetches = {}
+    for number, name in enumerate(FETCHED):
+        fetches[name] = pltpu.make_async_copy(getattr(r, name + "_hbm"), getattr(r, name), r.fetch.at[number])
+        fetches[name].start()
+
+    def fetched(*names):
+        for name in names:
+            fetches[name].wait()
+
     stations, convs = Stations(place, r), Convs(place, r)
+    fetched("obs", "target", "cell")
     stations.route()
+    fetched("cotangent")
     r.cot[8:40, 0:32] = r.cotangent[...]
     halo_cot, halo_hid = Halo(place, r, 0, r.cot), Halo(place, r, 1, r.hid.at[0])
     finish_greeting()
     stations.send()
-    halo_cot.start()
+    fetched("base", "embed")
     stations.receive()
     halo_hid.start()
-    halo_cot.end()
-    convs.spread_grad(2, (0, 48, 4))
-    fetch.wait()
+    halo_cot.start()
+    fetched("weights")
     halo_hid.end()
     convs.activate(0, (0, 48, 4))
     convs.forward(0, (2, 46, 11))
     convs.activate(1, (2, 46, 4))
     convs.forward(1, (4, 44, 10))
+    halo_cot.end()
+    convs.spread_grad(2, (0, 48, 4))
     convs.activate(2, (4, 44, 4))
     convs.forward(2, (8, 40, 16), 32)
 
-    sums = {layer: KernelSum(place, layer, r).steps for layer in range(3)}
+    sums = {layer: KernelSum(place, layer, r).steps for layer in (1, 2)}
+    sums[0] = PlaneSum(place, 0, r).steps
     sums["e"] = EmbedSum(place, r).steps
 
     def step(*which):
@@ -489,22 +547,18 @@
 
     convs.kernel(2)
     step(2)
-    convs.back(2, (4, 24, 10))
-    step(2)
-    convs.back(2, (24, 44, 10))
+    convs.back(2, (4, 44, 10))
     step(2)
     convs.spread_grad(1, (4, 44, 4))
     convs.kernel(1)
-    step(2, 1)
-    convs.back(1, (6, 24, 9))
-    step(2, 1)
-    convs.back(1, (24, 42, 9))
+    step(1)
+    convs.back(1, (6, 42, 9))
     step(2, 1)
     convs.spread_grad(0, (6, 42, 4))
     convs.kernel(0)
-    step(2, 1, 0)
+    step(0)
     convs.back(0, (8, 40, 16), 32)
-    step(2, 1, 0)
+    step(0, 2, 1)
     grad_low = low(r.base_grad[...].reshape(1024, 256))
     first, second = stations.gradient(grad_low)
     total = first + second
@@ -512,7 +566,7 @@
         r.e_part[half] = low(total[:, half * 128 : half * 128 + 128]).reshape(4, 32, 128)
     step("e")
     while any(sums.values()):
-        step(*[name for name in (1, 0, "e") if sums[name]])
+        step(*[name for name in ("e", 0, 2, 1) if sums[name]])
 
 
 SUM_SCRATCH = dict(
@@ -528,22 +582,32 @@
     e_sib=pltpu.VMEM((4, 32, 128), BF),
     e_own=pltpu.VMEM((4, 32, 128), BF),
     e_in=pltpu.VMEM((3, 32, 128), BF),
-    e_y=pltpu.VMEM((4, 32, 128), BF),
-    e_x=pltpu.VMEM((4, 32, 128), BF),
+    e_plane=pltpu.VMEM((16, 32, 128), BF),
+    e_plane_send=pltpu.SemaphoreType.DMA,
+    e_plane_recv=pltpu.SemaphoreType.DMA,
+    p_in=pltpu.VMEM((3, 15, 48, 128), BF),
+    p_send=pltpu.SemaphoreType.DMA((2, 3)),
+    p_recv=pltpu.SemaphoreType.DMA((2, 3)),
     e_res=pltpu.VMEM((32, 128), BF),
     send=pltpu.SemaphoreType.DMA((3, 3, 5, 3)),
     recv=pltpu.SemaphoreType.DMA((3, 3, 5, 3)),
     swap_send=pltpu.SemaphoreType.DMA((3, 2)),
     swap_recv=pltpu.SemaphoreType.DMA((3, 2)),
-    e_send=pltpu.SemaphoreType.DMA((4, 3)),
-    e_recv=pltpu.SemaphoreType.DMA((4, 3)),
+    e_send=pltpu.SemaphoreType.DMA((2, 3)),
+    e_recv=pltpu.SemaphoreType.DMA((2, 3)),
     e_swap_send=pltpu.SemaphoreType.DMA((2,)),
     e_swap_recv=pltpu.SemaphoreType.DMA((2,)),
 )
 SCRATCH = dict(
     SUM_SCRATCH,
     weights=pltpu.VMEM((3, 9, 256, 256), BF),
-    fetch=pltpu.SemaphoreType.DMA,
+    base=pltpu.VMEM((32, 32, 256), BF),
+    cotangent=pltpu.VMEM((32, 32, 256), BF),
+    obs=pltpu.VMEM((512, 128), BF),
+    embed=pltpu.VMEM((128, 256), BF),
+    target=pltpu.VMEM((1, 512), jnp.int32),
+    cell=pltpu.VMEM((1, 512), jnp.int32),
+    fetch=pltpu.SemaphoreType.DMA((7,)),
     st_out=pltpu.VMEM((DEVICES, 16, 128), BF),
     st_in=pltpu.VMEM((DEVICES, 16, 128), BF),
     st_send=pltpu.SemaphoreType.DMA,
@@ -560,16 +624,65 @@
     halo_send=pltpu.SemaphoreType.DMA((2, 8)),
     halo_recv=pltpu.SemaphoreType.DMA((2, 8)),
 )
-INPUTS = ("base", "obs", "meta", "embed", "weights_hbm", "cotangent")
+FETCHED = ("target", "cell", "obs", "base", "cotangent", "embed", "weights")
+INPUTS = ("base_hbm", "obs_hbm", "target_hbm", "cell_hbm", "count", "embed_hbm", "weights_hbm", "cotangent_hbm")
 OUTPUTS = ("block_out", "base_grad", "out", "e_out")
+
+
+CHUNKS = 9
+
+
+def finish_kernel(total, e_total, block, grad, conv_grads, embed_grad, block_out, base_grad, wide, e_wide, sems):
+    scale = 1.0 / math.sqrt(131072)
+    copies = [
+        pltpu.make_async_copy(block, block_out, sems.at[CHUNKS]),
+        pltpu.make_async_copy(grad, base_grad, sems.at[CHUNKS + 1]),
+    ]
+    for copy in copies:
+        copy.start()
+    for chunk in range(CHUNKS):
+        wide[chunk] = f32(total[chunk]) * scale
+        copies.append(pltpu.make_async_copy(wide.at[chunk], conv_grads.at[chunk], sems.at[chunk]))
+        copies[-1].start()
+    e_wide[...] = f32(e_total[...]) * scale
+    copies.append(pltpu.make_async_copy(e_wide, embed_grad, sems.at[CHUNKS + 2]))
+    copies[-1].start()
+    for copy in copies:
+        copy.wait()
+
+
+def finish(total, e_total, block, grad):
+    vmem, anywhere = pl.BlockSpec(memory_space=pltpu.VMEM), pl.BlockSpec(memory_space=pltpu.HBM)
+    size = 6912 // CHUNKS
+    return pl.pallas_call(
+        finish_kernel,
+        out_shape=[
+            jax.ShapeDtypeStruct((CHUNKS, size, 256), F32),
+            jax.ShapeDtypeStruct((128, 256), F32),
+            jax.ShapeDtypeStruct((32, 32, 256), BF),
+            jax.ShapeDtypeStruct((32, 32, 256), F32),
+        ],
+        in_specs=[vmem] * 4,
+        out_specs=[anywhere] * 4,
+        scratch_shapes=[
+            pltpu.VMEM((CHUNKS, size, 256), F32),
+            pltpu.VMEM((128, 256), F32),
+            pltpu.SemaphoreType.DMA((CHUNKS + 3,)),
+        ],
+        compiler_params=pltpu.CompilerParams(vmem_limit_bytes=16 * 2**20),
+        name="finish",
+    )(total, e_total, block, grad)
+
+
+def stay(array):
+    return pltpu.with_memory_space_constraint(array, pltpu.HBM)
 
 
 def local(
     base, observations, destination, cell_index, shard_counts, embed_weight, conv_weights, cotangent
 ):
-    live = jnp.arange(512, dtype=jnp.int32) < shard_counts[0]
-    meta = jnp.concatenate([destination, jnp.where(live, cell_index, -1)[:, None]], axis=1)
-    vmem, anywhere = pl.BlockSpec(memory_space=pltpu.VMEM), pl.BlockSpec(memory_space=pl.ANY)
+    target, cell = destination.reshape(1, 512), cell_index.reshape(1, 512)
+    vmem, hbm = pl.BlockSpec(memory_space=pltpu.VMEM), pl.BlockSpec(memory_space=pltpu.HBM)
     names = INPUTS + OUTPUTS + tuple(SCRATCH)
     block_out, base_grad, total, e_total = pl.pallas_call(
         lambda *refs: whole_kernel(names, *refs),
@@ -579,18 +692,21 @@
             jax.ShapeDtypeStruct((3, 3, 4, 4, 48, 256), BF),
             jax.ShapeDtypeStruct((4, 32, 256), BF),
         ],
-        in_specs=[vmem, vmem, vmem, vmem, anywhere, vmem],
+        in_specs=[hbm, hbm, hbm, hbm, pl.BlockSpec(memory_space=pltpu.SMEM), hbm, hbm, hbm],
         out_specs=[vmem, vmem, vmem, vmem],
         scratch_shapes=list(SCRATCH.values()),
         compiler_params=pltpu.CompilerParams(
-            collective_id=0, has_side_effects=True, vmem_limit_bytes=60 * 2**20
+            collective_id=0, has_side_effects=True, vmem_limit_bytes=47 * 2**20
         ),
         name="station_block",
-    )(base, observations, meta, embed_weight, conv_weights, cotangent)
-    scale = 1.0 / math.sqrt(131072)
-    conv_grads = total.reshape(3, 9, 256, 256).astype(F32) * scale
-    embed_grad = e_total.reshape(128, 256).astype(F32) * scale
-    return (block_out, base_grad, conv_grads, embed_grad)
+    )(
+        stay(base), stay(observations), stay(target), stay(cell), shard_counts, stay(embed_weight),
+        stay(conv_weights), stay(cotangent),
+    )
+    conv_grads, embed_grad, block_out, base_grad = finish(
+        total.reshape(CHUNKS, 6912 // CHUNKS, 256), e_total.reshape(128, 256), block_out, base_grad
+    )
+    return (block_out, base_grad, conv_grads.reshape(3, 9, 256, 256), embed_grad)
 
 
 def solution(mesh):

time: 113 us -> 93.2 us (0.82)
  Pallas kernels: 101 us -> 91.6 us
  other arithmetic: 8.15 us -> 0 us
  local copies, waits for them, and re-layouts: 2.64 us -> 0 us
    pallas_call x1, Pallas kernels: 101 us -> 88.1 us  [local(): pl.pallas_call(lambda *refs: whole_kernel(names, *refs), out_shape=[jax.S...]
    mul x2 -> x0, other arithmetic: 6.77 us -> none  [the longest x1 6.1 us: local(): conv_grads = total.reshape(3, 9, 256, 256).astype(F32) * scale]
    pallas_call x0 -> x1, Pallas kernels: none -> 3.5 us  [finish(): pl.pallas_call(finish_kernel, out_shape=[jax.ShapeDtypeStruct((CHUNKS, si...]
    unnamed x8 -> x0, local copies, waits for them, and re-layouts: 1.78 us -> none
where the time goes in v1:
time: 93.2 us; the launch traced here: 93.1 us
  Pallas kernels  91.6 us (98%)
  between operations  1.45 us (2%)
    pallas_call x1, Pallas kernels, local(): pl.pallas_call(lambda *refs: whole_kernel(names, *refs), out_shape=[jax.S...  88.1 us
    pallas_call x1, Pallas kernels, finish(): pl.pallas_call(finish_kernel, out_shape=[jax.ShapeDtypeStruct((CHUNKS, si...  3.5 us

profile of v1, /device:TPU:1, one launch (start us, length us, event | category | flops | bytes accessed | tf_op | source)
XLA Modules:
  0.0 93.1 jit_solution(16486774796017941765)
XLA Ops:
  1.3 88.1 %station_block.1 = (bf16[32,32,256]{2,1,0:T(8,128)(2,1)S(1)}, f32[32,32,256]{2,1,0:T(8,128)S(1)}, bf16[3,3,4,4,48,256]{5,4,3,2,1,0:T(8,128)(2,1)S(1)}, bf16[4,32,256]{2,1,0:T(8,128)(2,1)S(1)}) custom-call(bf16[32,32,256]{2,1,0:T(8,128)(2,1)} %refs_0_.1, bf16[512,128]{1,0:T(8,128)(2,1)} %refs_1_.1, s32[1,512]{1,0:T(1,128)} %bitcast.7, s32[1,512]{1,0:T(1,128)} %bitcast.8, ...), custom_call_target="tpu_custom_call" | custom-call | tf_op jit(solution)/shard_map/station_block/pallas_call | solution.py:687
  89.4 3.5 %finish.1 = (f32[9,768,256]{2,1,0:T(8,128)}, f32[128,256]{1,0:T(8,128)}, bf16[32,32,256]{2,1,0:T(8,128)(2,1)}, f32[32,32,256]{2,1,0:T(8,128)}) custom-call(bf16[9,768,256]{2,1,0:T(8,128)(2,1)S(1)} %bitcast.5, bf16[128,256]{1,0:T(8,128)(2,1)S(1)} %bitcast.6, bf16[32,32,256]{2,1,0:T(8,128)(2,1)S(1)} %get-tuple-element.14.block, ...), custom_call_target="tpu_custom_call" | custom-call | tf_op jit(solution)/shard_map/finish/pallas_call | solution.py:657

commit v2 on v1

--- a/solution.py
+++ b/solution.py
@@ -63,17 +63,17 @@
         self.place, self.layer, self.refs = place, layer, refs
         self.lanes = part_of(place.core, 128)
         self.steps = [
-            self.swap, self.scatter_a, self.scatter_b, self.share_c, self.gather_b, self.gather_a,
+            self.scatter_a, self.scatter_b, self.share_c, self.gather_b, self.gather_a,
             self.swap_back, self.end,
         ]
 
-    def swap_copy(self, back):
+    def swap_copy(self, back, group):
         r, l, core = self.refs, self.layer, self.place.core
-        sems = r.swap_send.at[l, back], r.swap_recv.at[l, back]
+        sems = r.swap_send.at[l, back, group], r.swap_recv.at[l, back, group]
         if back:
-            mine = r.out.at[l, :, :, :, :, self.lanes]
+            mine = r.out.at[l, group, :, :, :, self.lanes]
             return remote(mine, mine, sems, self.place.sibling())
-        return remote(r.part.at[l, 1 - core], r.sib.at[l], sems, self.place.sibling())
+        return remote(r.part.at[l, 1 - core, group], r.sib.at[l, group], sems, self.place.sibling())
 
     def copies(self, phase):
         r, l = self.refs, self.layer
@@ -102,13 +102,13 @@
         for copy in self.copies(phase):
             copy.wait()
 
-    def swap(self):
-        self.swap_copy(0).start()
+    def swap(self, group):
+        self.swap_copy(0, group).start()
 
     def scatter_a(self):
         r, l, core = self.refs, self.layer, self.place.core
-        self.swap_copy(0).wait()
         for group in range(3):
+            self.swap_copy(0, group).wait()
             r.a_own[l, group] = low(f32(r.part[l, core, group]) + f32(r.sib[l, group]))
         self.start(0)
 
@@ -151,16 +151,19 @@
 
     def swap_back(self):
         self.wait(4)
-        self.swap_copy(1).start()
+        for group in range(3):
+            self.swap_copy(1, group).start()
 
     def end(self):
-        self.swap_copy(1).wait()
+        for group in range(3):
+            self.swap_copy(1, group).wait()
 
 
 class PlaneSum(KernelSum):
-    def __init__(self, place, layer, refs):
+    def __init__(self, place, layer, refs, slot):
         super().__init__(place, layer, refs)
-        self.steps = [self.swap, self.scatter, self.share_c, self.gather_b, self.swap_back, self.end]
+        self.slot = slot
+        self.steps = [self.scatter, self.share_c, self.gather_b, self.swap_back, self.end]
 
     def pieces(self, group):
         a, b, _ = ORDERS[group]
@@ -168,30 +171,28 @@
             to = {a: self.place.other(a, step // 4), b: self.place.other(b, step % 4)}
             yield step - 1, to[a], to[b], self.place.device(**to)
 
-    def plane_wait(self, phase):
-        r = self.refs
-        for group in range(3):
-            whole = r.p_in.at[group]
-            remote(whole, whole, (r.p_send.at[phase, group], r.p_recv.at[phase, group]), self.place.sibling()).wait()
+    def plane_wait(self, phase, group):
+        r, whole = self.refs, self.refs.p_in.at[self.slot, group]
+        sems = r.p_send.at[self.slot, phase, group], r.p_recv.at[self.slot, phase, group]
+        remote(whole, whole, sems, self.place.sibling()).wait()
 
     def scatter(self):
         r, l, core = self.refs, self.layer, self.place.core
-        self.swap_copy(0).wait()
         for group in range(3):
+            self.swap_copy(0, group).wait()
             r.a_own[l, group] = low(f32(r.part[l, core, group]) + f32(r.sib[l, group]))
-        for group in range(3):
-            sems = r.p_send.at[0, group], r.p_recv.at[0, group]
+            sems = r.p_send.at[self.slot, 0, group], r.p_recv.at[self.slot, 0, group]
             for slot, to_a, to_b, device in self.pieces(group):
                 piece = r.a_own.at[l, group, part_of(to_a * 4 + to_b, 48)]
-                remote(piece, r.p_in.at[group, slot], sems, device).start()
+                remote(piece, r.p_in.at[self.slot, group, slot], sems, device).start()
 
     def share_c(self):
         r, l = self.refs, self.layer
-        self.plane_wait(0)
         for group, (a, b, c) in enumerate(ORDERS):
+            self.plane_wait(0, group)
             total = f32(r.a_own[l, group, part_of(self.place.at[a] * 4 + self.place.at[b], 48)])
             for slot in range(15):
-                total += f32(r.p_in[group, slot])
+                total += f32(r.p_in[self.slot, group, slot])
             r.c_all[l, group, self.place.at[c]] = low(total)
         self.start(2)
 
@@ -204,21 +205,22 @@
                 total += f32(r.c_all[l, group, index])
             mine = r.out.at[l, group, self.place.at[a], self.place.at[b], :, self.lanes]
             r.b_res[l, group, 0] = low(total)
-            sems = r.p_send.at[1, group], r.p_recv.at[1, group]
+            sems = r.p_send.at[self.slot, 1, group], r.p_recv.at[self.slot, 1, group]
             for _, _, _, device in self.pieces(group):
                 remote(r.b_res.at[l, group, 0], mine, sems, device).start()
             mine[...] = low(total)
 
     def swap_back(self):
-        self.plane_wait(1)
-        self.swap_copy(1).start()
+        for group in range(3):
+            self.plane_wait(1, group)
+            self.swap_copy(1, group).start()
 
 
 class EmbedSum(KernelSum):
     def __init__(self, place, refs):
         self.place, self.refs = place, refs
         self.lanes = part_of(place.core, 128)
-        self.steps = [self.swap, self.scatter, self.share, self.gather, self.swap_back, self.end]
+        self.steps = [self.scatter, self.share, self.gather, self.swap_back, self.end]
 
     def swap_copy(self, back):
         r, core = self.refs, self.place.core
@@ -236,6 +238,12 @@
             sems = r.e_send.at[phase, step - 1], r.e_recv.at[phase, step - 1]
             result.append(remote(src, dst, sems, self.place.device(z=to)))
         return result
+
+    def swap(self):
+        self.swap_copy(0).start()
+
+    def end(self):
+        self.swap_copy(1).wait()
 
     def scatter(self):
         r = self.refs
@@ -375,7 +383,15 @@
             picks = low(jnp.where(cells == cell_row, 1.0, 0.0))
             placed = jnp.dot(picks, embedded, preferred_element_type=F32).reshape(8, 32, 256)
             own = slice(part * 8, part * 8 + 8)
-            r.hid[0, part * 8 + 8 : part * 8 + 16, 0:32] = low(f32(r.base[own]) + placed)
+            r.hid[0][part * 8 + 8 : part * 8 + 16, 0:32] = low(f32(r.base[own]) + placed)
+
+    def embed_part(self):
+        r = self.refs
+        grad_low = low(r.base_grad[...].reshape(1024, 256))
+        first, second = self.gradient(grad_low)
+        total = first + second
+        for half in range(2):
+            r.e_part[half] = low(total[:, half * 128 : half * 128 + 128]).reshape(4, 32, 128)
 
     def gradient(self, grad_low):
         r = self.refs
@@ -403,33 +419,48 @@
     def __init__(self, place, refs):
         self.place, self.refs = place, refs
 
-    def inside(self, first, rows):
-        row = lax.broadcasted_iota(jnp.int32, (rows, EXT, 256), 0) + (first - 8 + self.place.row * 32)
-        col = lax.broadcasted_iota(jnp.int32, (rows, EXT, 256), 1)
+    def spread(self, value_of, out, spacing, sign):
+        col = lax.broadcasted_iota(jnp.int32, (EXT, 256), 0)
         col = jnp.where(col < 40, col, col - EXT) + self.place.col * 32
-        return (row >= 0) & (row < 256) & (col >= 0) & (col < 512)
-
-    def spread(self, value_of, out, spacing, sign, rows):
+        in_cols = f32((col >= 0) & (col < 512))
+
+        def one(row, size):
+            values = value_of(row, size)
+            for k in range(size):
+                grid_row = row + k - 8 + self.place.row * 32
+                in_row = jnp.where((grid_row >= 0) & (grid_row < 256), 1.0, 0.0)
+                value = jnp.where(in_cols * in_row > 0.0, values[k], 0.0)
+                out[1, row + k] = low(value)
+                out[1 - sign, row + k] = low(pltpu.roll(value, spacing, 0))
+                out[1 + sign, row + k] = low(pltpu.roll(value, EXT - spacing, 0))
+
+        return one
+
+    def along(self, rows, work, behind=None):
         first, last, size = rows
 
         def one(step, carry):
             row = first + step * size
-            value = jnp.where(self.inside(row, size), value_of(row, size), 0.0)
-            out[1, pl.ds(row, size)] = low(value)
-            out[1 - sign, pl.ds(row, size)] = low(jnp.roll(value, spacing, axis=1))
-            out[1 + sign, pl.ds(row, size)] = low(jnp.roll(value, -spacing, axis=1))
+            if behind is not None:
+                behind(row - size, size)
+            work(row, size)
             return carry
 
-        lax.fori_loop(0, (last - first) // size, one, 0)
-
-    def activate(self, layer, rows):
-        hid = self.refs.hid.at[layer]
+        if behind is None:
+            lax.fori_loop(0, (last - first) // size, one, 0)
+        else:
+            work(first, size)
+            lax.fori_loop(1, (last - first) // size, one, 0)
+            behind(last - size, size)
+
+    def activation(self, layer):
+        hid = self.refs.hid[layer]
 
         def value(row, size):
             x = f32(hid[pl.ds(row, size)])
             return x * sigmoid(x)
 
-        self.spread(value, self.refs.act.at[layer], 2**layer, 1, rows)
+        return self.spread(value, self.refs.act[layer], 2**layer, 1)
 
     def taps(self, source, weights, row, size, width, spacing, sign, turned):
         total = None
@@ -442,58 +473,55 @@
         return total.reshape(size, width, 256)
 
     def forward(self, layer, rows, width=EXT):
-        r, (first, last, size) = self.refs, rows
-
-        def one(step, carry):
-            row = first + step * size
-            update = self.taps(r.act.at[layer], r.weights.at[layer], row, size, width, 2**layer, 1, False)
-            result = low(f32(r.hid[layer, pl.ds(row, size), 0:width]) + update)
+        r = self.refs
+
+        def work(row, size):
+            update = self.taps(r.act[layer], r.weights.at[layer], row, size, width, 2**layer, 1, False)
+            result = low(f32(r.hid[layer][pl.ds(row, size), 0:width]) + update)
             if layer == 2:
                 r.block_out[pl.ds(row - 8, size)] = result
             else:
-                r.hid[layer + 1, pl.ds(row, size)] = result
-            return carry
-
-        lax.fori_loop(0, (last - first) // size, one, 0)
-
-    def kernel(self, layer):
+                r.hid[layer + 1][pl.ds(row, size)] = result
+
+        self.along(rows, work, None if layer == 2 else self.activation(layer + 1))
+
+    def kernel(self, layer, then):
         r, spacing = self.refs, 2**layer
-        grad = r.grad_low[1, 8:40, 0:32].reshape(1024, 256)
-
-        def one(j, carry):
-            for i in range(3):
-                row = 8 + (i - 1) * spacing
-                cells = r.act[layer, j, row : row + 32, 0:32].reshape(1024, 256)
+        grad = r.grad_low[layer % 2][1, 8:40, 0:32].reshape(1024, 256)
+        for i in range(3):
+            row = 8 + (i - 1) * spacing
+
+            def one(j, carry):
+                cells = r.act[layer][j, row : row + 32, 0:32].reshape(1024, 256)
                 total = lax.dot_general(cells, grad, (((0,), (0,)), ((), ())), preferred_element_type=F32)
                 for half in range(2):
                     r.part[layer, half, i, part_of(j, 256)] = low(total[:, half * 128 : half * 128 + 128])
-            return carry
-
-        lax.fori_loop(0, 3, one, 0)
+                return carry
+
+            lax.fori_loop(0, 3, one, 0)
+            then(i)
 
     def back(self, layer, rows, width=EXT):
-        r, (first, last, size) = self.refs, rows
-
-        def one(step, carry):
-            row = first + step * size
-            update = self.taps(r.grad_low, r.weights.at[layer], row, size, width, 2**layer, -1, True)
+        r = self.refs
+
+        def work(row, size):
+            update = self.taps(r.grad_low[layer % 2], r.weights.at[layer], row, size, width, 2**layer, -1, True)
             before = f32(r.cot[pl.ds(row, size)]) if layer == 2 else r.grad[pl.ds(row, size), 0:width]
-            result = before + update * silu_slope(f32(r.hid[layer, pl.ds(row, size), 0:width]))
+            result = before + update * silu_slope(f32(r.hid[layer][pl.ds(row, size), 0:width]))
             if layer == 0:
                 r.base_grad[pl.ds(row - 8, size)] = result
             else:
                 r.grad[pl.ds(row, size)] = result
-            return carry
-
-        lax.fori_loop(0, (last - first) // size, one, 0)
-
-    def spread_grad(self, layer, rows):
+
+        self.along(rows, work, self.gradient(layer - 1) if layer else None)
+
+    def gradient(self, layer):
         r = self.refs
 
         def value(row, size):
             return f32(r.cot[pl.ds(row, size)]) if layer == 2 else r.grad[pl.ds(row, size)]
 
-        self.spread(value, r.grad_low, 2**layer, -1, rows)
+        return self.spread(value, r.grad_low[layer % 2], 2**layer, -1)
 
 
 class Refs:
@@ -519,56 +547,63 @@
     stations.route()
     fetched("cotangent")
     r.cot[8:40, 0:32] = r.cotangent[...]
-    halo_cot, halo_hid = Halo(place, r, 0, r.cot), Halo(place, r, 1, r.hid.at[0])
+    halo_cot, halo_hid = Halo(place, r, 0, r.cot), Halo(place, r, 1, r.hid[0])
     finish_greeting()
     stations.send()
+    halo_cot.start()
     fetched("base", "embed")
     stations.receive()
     halo_hid.start()
-    halo_cot.start()
     fetched("weights")
+    halo_cot.end()
+    convs.along((0, 48, 4), convs.gradient(2))
     halo_hid.end()
-    convs.activate(0, (0, 48, 4))
+    convs.along((0, 48, 4), convs.activation(0))
     convs.forward(0, (2, 46, 11))
-    convs.activate(1, (2, 46, 4))
     convs.forward(1, (4, 44, 10))
-    halo_cot.end()
-    convs.spread_grad(2, (0, 48, 4))
-    convs.activate(2, (4, 44, 4))
-    convs.forward(2, (8, 40, 16), 32)
-
-    sums = {layer: KernelSum(place, layer, r).steps for layer in (1, 2)}
-    sums[0] = PlaneSum(place, 0, r).steps
-    sums["e"] = EmbedSum(place, r).steps
-
-    def step(*which):
-        for name in which:
-            sums[name].pop(0)()
-
-    convs.kernel(2)
-    step(2)
+    sums = [KernelSum(place, 0, r), KernelSum(place, 1, r), KernelSum(place, 2, r), EmbedSum(place, r)]
+
+    def step(which):
+        sums[which].steps.pop(0)()
+
+    convs.kernel(2, sums[2].swap)
     convs.back(2, (4, 44, 10))
     step(2)
-    convs.spread_grad(1, (4, 44, 4))
-    convs.kernel(1)
+    convs.kernel(1, sums[1].swap)
+    convs.back(1, (6, 42, 9))
     step(1)
-    convs.back(1, (6, 42, 9))
-    step(2, 1)
-    convs.spread_grad(0, (6, 42, 4))
-    convs.kernel(0)
+    step(2)
+    convs.kernel(0, sums[0].swap)
+    convs.forward(2, (8, 40, 16), 32)
     step(0)
+    step(2)
+    step(1)
     convs.back(0, (8, 40, 16), 32)
-    step(0, 2, 1)
-    grad_low = low(r.base_grad[...].reshape(1024, 256))
-    first, second = stations.gradient(grad_low)
-    total = first + second
-    for half in range(2):
-        r.e_part[half] = low(total[:, half * 128 : half * 128 + 128]).reshape(4, 32, 128)
-    step("e")
-    while any(sums.values()):
-        step(*[name for name in ("e", 0, 2, 1) if sums[name]])
-
-
+    stations.embed_part()
+    sums[3].swap()
+    step(0)
+    step(3)
+    step(2)
+    step(1)
+    step(0)
+    step(3)
+    step(2)
+    step(1)
+    step(0)
+    step(3)
+    step(2)
+    step(1)
+    step(0)
+    step(3)
+    step(2)
+    step(1)
+    step(0)
+    step(3)
+    step(1)
+    step(0)
+
+
+PLANES = 1
 SUM_SCRATCH = dict(
     part=pltpu.VMEM((3, 2, 3, 768, 128), BF),
     sib=pltpu.VMEM((3, 3, 768, 128), BF),
@@ -585,14 +620,14 @@
     e_plane=pltpu.VMEM((16, 32, 128), BF),
     e_plane_send=pltpu.SemaphoreType.DMA,
     e_plane_recv=pltpu.SemaphoreType.DMA,
-    p_in=pltpu.VMEM((3, 15, 48, 128), BF),
-    p_send=pltpu.SemaphoreType.DMA((2, 3)),
-    p_recv=pltpu.SemaphoreType.DMA((2, 3)),
+    p_in=pltpu.VMEM((PLANES, 3, 15, 48, 128), BF),
+    p_send=pltpu.SemaphoreType.DMA((PLANES, 2, 3)),
+    p_recv=pltpu.SemaphoreType.DMA((PLANES, 2, 3)),
     e_res=pltpu.VMEM((32, 128), BF),
     send=pltpu.SemaphoreType.DMA((3, 3, 5, 3)),
     recv=pltpu.SemaphoreType.DMA((3, 3, 5, 3)),
-    swap_send=pltpu.SemaphoreType.DMA((3, 2)),
-    swap_recv=pltpu.SemaphoreType.DMA((3, 2)),
+    swap_send=pltpu.SemaphoreType.DMA((3, 2, 3)),
+    swap_recv=pltpu.SemaphoreType.DMA((3, 2, 3)),
     e_send=pltpu.SemaphoreType.DMA((2, 3)),
     e_recv=pltpu.SemaphoreType.DMA((2, 3)),
     e_swap_send=pltpu.SemaphoreType.DMA((2,)),
@@ -615,9 +650,9 @@
     rows=pltpu.VMEM((1024, 128), BF),
     cell_col=pltpu.VMEM((1024, 1), F32),
     cot=pltpu.VMEM((EXT, EXT, 256), BF),
-    hid=pltpu.VMEM((3, EXT, EXT, 256), BF),
-    act=pltpu.VMEM((3, 3, EXT, EXT, 256), BF),
-    grad_low=pltpu.VMEM((3, EXT, EXT, 256), BF),
+    hid=[pltpu.VMEM((EXT, EXT, 256), BF)] * 3,
+    act=[pltpu.VMEM((3, EXT, EXT, 256), BF)] * 3,
+    grad_low=[pltpu.VMEM((3, EXT, EXT, 256), BF)] * 2,
     grad=pltpu.VMEM((EXT, EXT, 256), F32),
     strip_out=pltpu.VMEM((2, 768, 256), BF),
     strip_in=pltpu.VMEM((2, 768, 256), BF),

time: 93.2 us -> 90.2 us (0.968)
  Pallas kernels: 91.6 us -> 88.6 us
    pallas_call x1, Pallas kernels: 88.1 us -> 85.1 us  [local(): pl.pallas_call(lambda *refs: whole_kernel(names, *refs), out_shape=[jax.S...]
where the time goes in v2:
time: 90.2 us; the launch traced here: 90.1 us
  Pallas kernels  88.6 us (98%)
  between operations  1.45 us (2%)
    pallas_call x1, Pallas kernels, local(): pl.pallas_call(lambda *refs: whole_kernel(names, *refs), out_shape=[jax.S...  85.1 us
    pallas_call x1, Pallas kernels, finish(): pl.pallas_call(finish_kernel, out_shape=[jax.ShapeDtypeStruct((CHUNKS, si...  3.5 us

profile of v2, /device:TPU:1, one launch (start us, length us, event | category | flops | bytes accessed | tf_op | source)
XLA Modules:
  0.0 90.1 jit_solution(411811125389548900)
XLA Ops:
  1.3 85.1 %station_block.1 = (bf16[32,32,256]{2,1,0:T(8,128)(2,1)S(1)}, f32[32,32,256]{2,1,0:T(8,128)S(1)}, bf16[3,3,4,4,48,256]{5,4,3,2,1,0:T(8,128)(2,1)S(1)}, bf16[4,32,256]{2,1,0:T(8,128)(2,1)S(1)}) custom-call(bf16[32,32,256]{2,1,0:T(8,128)(2,1)} %refs_0_.1, bf16[512,128]{1,0:T(8,128)(2,1)} %refs_1_.1, s32[1,512]{1,0:T(1,128)} %bitcast.7, s32[1,512]{1,0:T(1,128)} %bitcast.8, ...), custom_call_target="tpu_custom_call" | custom-call | tf_op jit(solution)/shard_map/station_block/pallas_call | solution.py:722
  86.4 3.5 %finish.1 = (f32[9,768,256]{2,1,0:T(8,128)}, f32[128,256]{1,0:T(8,128)}, bf16[32,32,256]{2,1,0:T(8,128)(2,1)}, f32[32,32,256]{2,1,0:T(8,128)}) custom-call(bf16[9,768,256]{2,1,0:T(8,128)(2,1)S(1)} %bitcast.5, bf16[128,256]{1,0:T(8,128)(2,1)S(1)} %bitcast.6, bf16[32,32,256]{2,1,0:T(8,128)(2,1)S(1)} %get-tuple-element.14.block, ...), custom_call_target="tpu_custom_call" | custom-call | tf_op jit(solution)/shard_map/finish/pallas_call | solution.py:692

commit v3 on v2

--- a/solution.py
+++ b/solution.py
@@ -559,18 +559,18 @@
     convs.along((0, 48, 4), convs.gradient(2))
     halo_hid.end()
     convs.along((0, 48, 4), convs.activation(0))
-    convs.forward(0, (2, 46, 11))
-    convs.forward(1, (4, 44, 10))
+    convs.forward(0, (2, 46, 22))
+    convs.forward(1, (4, 44, 20))
     sums = [KernelSum(place, 0, r), KernelSum(place, 1, r), KernelSum(place, 2, r), EmbedSum(place, r)]
 
     def step(which):
         sums[which].steps.pop(0)()
 
     convs.kernel(2, sums[2].swap)
-    convs.back(2, (4, 44, 10))
+    convs.back(2, (4, 44, 20))
     step(2)
     convs.kernel(1, sums[1].swap)
-    convs.back(1, (6, 42, 9))
+    convs.back(1, (6, 42, 18))
     step(1)
     step(2)
     convs.kernel(0, sums[0].swap)

time: 90.2 us -> 88.2 us (0.978)
  Pallas kernels: 88.6 us -> 86.6 us
    pallas_call x1, Pallas kernels: 85.1 us -> 83.1 us  [local(): pl.pallas_call(lambda *refs: whole_kernel(names, *refs), out_shape=[jax.S...]
where the time goes in v3:
time: 88.2 us; the launch traced here: 88.1 us
  Pallas kernels  86.6 us (98%)
  between operations  1.45 us (2%)
    pallas_call x1, Pallas kernels, local(): pl.pallas_call(lambda *refs: whole_kernel(names, *refs), out_shape=[jax.S...  83.1 us
    pallas_call x1, Pallas kernels, finish(): pl.pallas_call(finish_kernel, out_shape=[jax.ShapeDtypeStruct((CHUNKS, si...  3.5 us

profile of v3, /device:TPU:1, one launch (start us, length us, event | category | flops | bytes accessed | tf_op | source)
XLA Modules:
  0.0 88.1 jit_solution(7326327325434235093)
XLA Ops:
  1.3 83.1 %station_block.1 = (bf16[32,32,256]{2,1,0:T(8,128)(2,1)S(1)}, f32[32,32,256]{2,1,0:T(8,128)S(1)}, bf16[3,3,4,4,48,256]{5,4,3,2,1,0:T(8,128)(2,1)S(1)}, bf16[4,32,256]{2,1,0:T(8,128)(2,1)S(1)}) custom-call(bf16[32,32,256]{2,1,0:T(8,128)(2,1)} %refs_0_.1, bf16[512,128]{1,0:T(8,128)(2,1)} %refs_1_.1, s32[1,512]{1,0:T(1,128)} %bitcast.7, s32[1,512]{1,0:T(1,128)} %bitcast.8, ...), custom_call_target="tpu_custom_call" | custom-call | tf_op jit(solution)/shard_map/station_block/pallas_call | solution.py:722
  84.4 3.5 %finish.1 = (f32[9,768,256]{2,1,0:T(8,128)}, f32[128,256]{1,0:T(8,128)}, bf16[32,32,256]{2,1,0:T(8,128)(2,1)}, f32[32,32,256]{2,1,0:T(8,128)}) custom-call(bf16[9,768,256]{2,1,0:T(8,128)(2,1)S(1)} %bitcast.5, bf16[128,256]{1,0:T(8,128)(2,1)S(1)} %bitcast.6, bf16[32,32,256]{2,1,0:T(8,128)(2,1)S(1)} %get-tuple-element.14.block, ...), custom_call_target="tpu_custom_call" | custom-call | tf_op jit(solution)/shard_map/finish/pallas_call | solution.py:692
